TPU v7x, 32 devices: a whole 2x2x4 slice. The times are simulated.
32 devices in a mesh: dev: 32 (over z, y, x, core).
Axes of the slice: x: 2, y: 2, z: 4, core: 2. Of those that a mesh axis runs over, the one named last changes fastest.
Arguments:
- samples: bfloat16 [1024, 201216], P('dev'), may hold values from -6 to 6
- input_gain: float32 [1024], P('dev'), may hold values from 0.3 to 4, as said below
Outputs:
- visibility: bfloat16 [768, 36, 2, 128, 128], P('dev')
Inputs may be any that keep to these rules, and one draw needn't show every extreme that they name: `input_gain`: positive gains, one for each input.
All inputs are finite; a program needn't handle non-finite values.
Results may differ from a plain program's by a relative error of at most 0.0071.
Values may be sent and summed in bfloat16 or wider, within the bound.
A program may use at most 320 MiB of HBM per device.

v0:
```python
import math

import jax
import jax.numpy as jnp
import numpy as np
from jax import lax
from jax.sharding import PartitionSpec as P

INPUTS = 1024
FRAME = 1536
TAPS = 4
BLOCK = 128


def pfb_window(frame_len, taps):
    total = taps * frame_len
    position = jnp.arange(total, dtype=jnp.int32).astype(jnp.float32)
    centred = (position - total / 2 + 0.5) / frame_len
    taper = 0.54 - 0.46 * jnp.cos(2.0 * math.pi * position / (total - 1))
    return (jnp.sinc(centred) * taper).reshape(taps, frame_len)


def dft_table(frame_len):
    channels = frame_len // 2
    sample_idx = jnp.arange(frame_len, dtype=jnp.int32)
    chan_idx = jnp.arange(channels, dtype=jnp.int32)
    phase = sample_idx[:, None] * chan_idx[None, :] % frame_len
    angle = 2.0 * math.pi / frame_len * phase.astype(jnp.float32)
    norm_factor = 1.0 / math.sqrt(frame_len)
    table = jnp.concatenate([jnp.cos(angle), -jnp.sin(angle)], axis=1) * norm_factor
    return table.astype(jnp.bfloat16)


def correlate(received):
    chans = received[0]
    count = chans.shape[0]
    inputs = chans.shape[1]
    width = chans.shape[2]
    spectra = width // 2
    nblk = inputs // BLOCK
    rows_np, cols_np = np.triu_indices(nblk)
    rows_idx = jnp.asarray(rows_np.astype(np.int32))
    cols_idx = jnp.asarray(cols_np.astype(np.int32))
    tiles = chans.reshape(count, nblk, BLOCK, width)
    left = jnp.take(tiles, rows_idx, axis=1)
    right = jnp.take(tiles, cols_idx, axis=1)
    turned = jnp.concatenate([-right[..., spectra:], right[..., :spectra]], axis=-1)
    real_part = jnp.einsum("kpis,kpjs->kpij", left, right, preferred_element_type=jnp.float32)
    imag_part = jnp.einsum("kpis,kpjs->kpij", left, turned, preferred_element_type=jnp.float32)
    stacked = jnp.stack([real_part, imag_part], axis=2) * (1.0 / spectra)
    return stacked.astype(jnp.bfloat16)


def local(samples, input_gain):
    num_dev = lax.axis_size("dev")
    local_inputs = samples.shape[0]
    frame_len = FRAME
    taps = TAPS
    channels = frame_len // 2
    spectra = samples.shape[1] // frame_len - taps + 1
    local_chans = channels // num_dev
    window = pfb_window(frame_len, taps)
    table = dft_table(frame_len)
    frames = samples.reshape(local_inputs, spectra + taps - 1, frame_len)
    acc = jnp.zeros((local_inputs, spectra, frame_len), jnp.float32)
    for tap in range(taps):
        acc = acc + window[tap][None, None, :] * frames[:, tap : tap + spectra, :].astype(
            jnp.float32
        )
    filtered = acc.astype(jnp.bfloat16).reshape(local_inputs * spectra, frame_len)
    spectrum = jnp.dot(filtered, table, preferred_element_type=jnp.float32)
    spectrum = (
        spectrum.reshape(local_inputs, spectra, 2, channels) * input_gain[:, None, None, None]
    )
    partial_power = jnp.sum(spectrum * spectrum, axis=(0, 1, 2))
    power = lax.psum(partial_power, "dev")
    level = 1.0 / jnp.sqrt(power / (INPUTS * spectra) + 1e-06)
    quantized = (spectrum * level[None, None, None, :]).astype(jnp.bfloat16)
    outgoing = quantized.reshape(local_inputs, spectra, 2, num_dev, local_chans)
    outgoing = outgoing.transpose(3, 4, 0, 2, 1).reshape(
        num_dev, local_chans, local_inputs, 2 * spectra
    )
    visibility = correlate(lax.all_to_all(outgoing, "dev", split_axis=0, concat_axis=2, tiled=True))
    return visibility


def solution(mesh):
    in_specs = (P("dev", None), P("dev"))
    out_specs = P("dev", None, None, None, None)
    return jax.shard_map(local, mesh=mesh, in_specs=in_specs, out_specs=out_specs, check_vma=False)
```

profile of v0, /device:TPU:0, one launch (start us, length us, event | category | flops | bytes accessed | tf_op | source)
XLA Modules:
  0.0 815.0 jit_solution(5972937322566629261)
XLA Ops:
  0.0 0.0 copy-start.2
  0.0 20.4 %sine_negate_fusion = (f32[1536,768]{0,1:T(8,128)}, f32[1536,768]{0,1:T(8,128)}) fusion(), kind=kLoop, calls=%fused_computation.33 | loop fusion | flops 11796480 | bytes 9437184 | tf_op jit(solution)/shard_map/neg | solution.py:30
  20.4 0.1 fusion.38
  20.5 12.6 %reshape.35 = bf16[32,131,1536]{2,1,0:T(8,128)(2,1)} reshape(bf16[32,201216]{1,0:T(8,128)(2,1)} %param.6) | data formatting | bytes 25755648 | tf_op jit(solution)/shard_map/reshape | solution.py:64
  33.1 7.2 fusion.27
  40.3 0.0 copy-done.2
  40.4 40.8 %multiply_reduce_fusion = (f32[768]{0:T(1024)S(1)}, f32[32,128,2,768]{3,1,2,0:T(8,128)}) fusion(f32[32]{0:T(128)S(1)} %copy-done.2, bf16[2,768,1536,1]{2,1,0,3:T(8,128)(2,1)} %bitcast.48, bf16[32,131,1536]{2,1,0:T(8,128)(2,1)} %reshape.35, f32[1536]{0:T(1024)S(1)} %get-tuple-element.9, f32[1536]{0:T(1024)S(1)} %get-tuple-element.10, ...), kind=kOutput, calls=%fused_computation.14 | convolution fusion | flops 19421724672 | bytes 80243840 | tf_op jit(solution)/shard_map/dot_general | solution.py:71
  81.2 42.2 %psum.7 = f32[768]{0:T(1024)S(1)} all-reduce(f32[768]{0:T(1024)S(1)} %get-tuple-element.12), channel_id=1, replica_groups=mesh['dev'=32] {'dev'}, use_global_device_ids=true, to_apply=%region_1.2 | all-reduce | flops 768 | bytes 6144 | tf_op jit(solution)/shard_map/psum | solution.py:76
  123.3 14.3 %multiply_convert_fusion = bf16[32,128,2,768]{3,1,2,0:T(8,128)(2,1)} fusion(f32[32,128,2,768]{3,1,2,0:T(8,128)} %get-tuple-element.13, f32[768]{0:T(1024)S(1)} %add_rsqrt_fusion, f32[32]{0:T(128)S(1)} %copy-done.2), kind=kLoop, calls=%fused_computation.13 | loop fusion | flops 18874368 | bytes 37751936 | tf_op jit(solution)/shard_map/convert_element_type | solution.py:78
  137.6 16.6 %copy.11 = bf16[32,128,2,768]{1,3,2,0:T(8,128)(2,1)} copy(bf16[32,128,2,768]{3,1,2,0:T(8,128)(2,1)} %multiply_convert_fusion) | data formatting | bytes 25165824 | tf_op jit(solution)/shard_map/convert_element_type | solution.py:78
  154.2 19.0 %copy.12 = bf16[32,24,32,2,128]{4,3,2,1,0:T(2,128)(2,1)} copy(bf16[32,24,32,2,128]{4,1,0,3,2:T(8,128)(2,1)} %bitcast.47) | data formatting | bytes 25165824 | tf_op jit(solution)/shard_map/transpose | solution.py:80
  173.2 0.0 copy-start
  173.2 0.0 copy-start.1
  173.2 20.5 %reshape.37 = bf16[32,24,32,256]{3,2,1,0:T(8,128)(2,1)} reshape(bf16[32,24,32,2,128]{4,3,2,1,0:T(2,128)(2,1)} %copy.12) | data formatting | bytes 25165824 | tf_op jit(solution)/shard_map/reshape | solution.py:80
  193.6 4.5 all-to-all-start
  198.2 0.0 copy-done
  198.2 0.0 copy-done.1
  198.2 278.7 %all-to-all-done = bf16[32,24,32,256]{3,2,1,0:T(8,128)(2,1)} async-done(((bf16[32,24,32,256]{3,2,1,0:T(8,128)(2,1)}), bf16[32,24,32,256]{3,2,1,0:T(8,128)(2,1)}, u32[]{:S(2)}, u32[]{:S(2)}) %all-to-all-start) | async-done | bytes 12582944 | tf_op jit(solution)/shard_map/all_to_all | solution.py:83
  476.9 10.6 %copy.13 = bf16[1,24,32,32,256]{4,3,2,1,0:T(8,128)(2,1)} copy(bf16[1,24,32,32,256]{4,3,1,2,0:T(8,128)(2,1)} %bitcast.8) | data formatting | bytes 25165824 | tf_op jit(solution)/shard_map/all_to_all | solution.py:83
  487.5 24.5 %gather_fusion.1 = bf16[36,24,128,256]{3,2,1,0:T(8,128)(2,1)} fusion(bf16[24,8,128,256]{3,2,1,0:T(8,128)(2,1)} %bitcast.44, s32[1024]{0:T(1024)S(1)} %pad_clamp_fusion), kind=kCustom, calls=%fused_computation.1.clone | custom fusion | bytes 113246352 | tf_op jit(solution)/shard_map/jit(_take)/gather | solution.py:46
  512.0 37.5 %copy.35 = bf16[36,24,128,256]{3,2,0,1:T(8,128)(2,1)} copy(bf16[36,24,128,256]{3,2,1,0:T(8,128)(2,1)} %gather_fusion.1) | data formatting | bytes 113246208 | tf_op jit(solution)/shard_map/jit(_take)/gather | solution.py:46
  549.5 37.0 %slice_negate_fusion = (bf16[24,36,128,128]{3,2,1,0:T(8,128)(2,1)}, bf16[24,36,128,128]{3,2,1,0:T(8,128)(2,1)}) fusion(bf16[24,36,128,256]{3,2,1,0:T(8,128)(2,1)} %bitcast.46), kind=kLoop, calls=%fused_computation.12 | loop fusion | flops 14155776 | bytes 113246208 | tf_op jit(solution)/shard_map/neg | solution.py:47
  586.5 23.6 %gather_fusion = bf16[36,24,128,256]{3,2,1,0:T(8,128)(2,1)} fusion(bf16[24,8,128,256]{3,2,1,0:T(8,128)(2,1)} %bitcast.45, s32[1024]{0:T(1024)S(1)} %pad_clamp_fusion.1), kind=kCustom, calls=%fused_computation.clone | custom fusion | bytes 113246352 | tf_op jit(solution)/shard_map/jit(_take)/gather | solution.py:45
  610.1 55.9 %fusion.8 = f32[24,36,1,128,128]{4,3,1,0,2:T(8,128)} fusion(bf16[36,24,128,256]{3,2,1,0:T(8,128)(2,1)} %gather_fusion.1, bf16[36,24,128,256]{3,2,1,0:T(8,128)(2,1)} %gather_fusion), kind=kOutput, calls=%fused_computation.16 | convolution fusion | flops 7247757312 | bytes 169869312 | tf_op jit(solution)/shard_map/kpis,kpjs->kpij/dot_general | solution.py:48
  666.1 56.1 %fusion.11 = f32[24,36,1,128,128]{4,3,1,0,2:T(8,128)} fusion(bf16[24,36,128,128]{3,2,1,0:T(8,128)(2,1)} %get-tuple-element.7, bf16[24,36,128,128]{3,2,1,0:T(8,128)(2,1)} %get-tuple-element.6, bf16[36,24,128,256]{3,2,1,0:T(8,128)(2,1)} %gather_fusion), kind=kOutput, calls=%fused_computation.17 | convolution fusion | flops 7361003520 | bytes 169869312 | tf_op jit(solution)/shard_map/kpis,kpjs->kpij/dot_general | solution.py:49
  722.2 54.9 %fusion = bf16[24,36,2,128,128]{4,3,1,0,2:T(8,128)(2,1)} fusion(f32[24,36,1,128,128]{4,3,1,0,2:T(8,128)} %fusion.11, f32[24,36,1,128,128]{4,3,1,0,2:T(8,128)} %fusion.8), kind=kLoop, calls=%fused_computation.3 | loop fusion | flops 84934656 | bytes 169869312 | tf_op jit(solution)/shard_map/convert_element_type | solution.py:51
  777.2 37.9 %copy.17 = bf16[24,36,2,128,128]{4,3,2,1,0:T(8,128)(2,1)} copy(bf16[24,36,2,128,128]{4,3,1,0,2:T(8,128)(2,1)} %fusion) | data formatting | bytes 113246208 | tf_op jit(solution)/shard_map/convert_element_type | solution.py:51
  (4 shorter events, 0.0 us)
Async XLA Ops:
  0.0 40.4 %copy-start.2 = (f32[32]{0:T(128)S(1)}, f32[32]{0:T(128)}, u32[]{:S(2)}) copy-start(f32[32]{0:T(128)} %param.7) | copy-start | bytes 388
  173.2 25.0 %copy-start = (s32[36]{0:T(128)S(1)}, s32[36]{0:T(128)}, u32[]{:S(2)}) copy-start(s32[36]{0:T(128)} %constant.116) | copy-start | bytes 436
  173.2 25.0 %copy-start.1 = (s32[36]{0:T(128)S(1)}, s32[36]{0:T(128)}, u32[]{:S(2)}) copy-start(s32[36]{0:T(128)} %constant.115) | copy-start | bytes 436
  193.6 283.2 %all-to-all-start = ((bf16[32,24,32,256]{3,2,1,0:T(8,128)(2,1)}), bf16[32,24,32,256]{3,2,1,0:T(8,128)(2,1)}, u32[]{:S(2)}, u32[]{:S(2)}) async-start(bf16[32,24,32,256]{3,2,1,0:T(8,128)(2,1)} %reshape.37), calls=%async_computation | async-start | bytes 25165824 | tf_op jit(solution)/shard_map/all_to_all | solution.py:83
where the time goes:
time: 816 us; the launch traced here: 815 us
  waiting for transfers between devices  279 us (34%)
  local copies, waits for them, and re-layouts  203 us (25%)
  matrix products  153 us (19%)
  other arithmetic  134 us (16%)
  blocking collectives  42.2 us (5%)
    all_to_all x1, waiting for transfers between devices, local(): lax.all_to_all(outgoing, 'dev', split_axis=0, concat_axis=2, tiled=True)  279 us
    gather x2, local copies, waits for them, and re-layouts, correlate(): right = jnp.take(tiles, cols_idx, axis=1)  62 us
    dot_general x1, matrix products, correlate(): jnp.einsum('kpis,kpjs->kpij', left, turned, preferred_element_type=jnp.fl...  56.1 us
    dot_general x1, matrix products, correlate(): jnp.einsum('kpis,kpjs->kpij', left, right, preferred_element_type=jnp.flo...  55.9 us
    convert_element_type x1, other arithmetic, correlate(): return stacked.astype(jnp.bfloat16)  54.9 us
    psum x1, blocking collectives, local(): power = lax.psum(partial_power, 'dev')  42.2 us
    dot_general x1, matrix products, local(): spectrum = jnp.dot(filtered, table, preferred_element_type=jnp.float32)  40.8 us
    convert_element_type x1, local copies, waits for them, and re-layouts, correlate(): return stacked.astype(jnp.bfloat16)  37.9 us
  transfers between devices with their start and end apart: 1, of which 1 were waited for; matrix products, arithmetic and copies ran while one was open for 0% of the time, Pallas kernels for 0%

commit v1 on v0

v1 whole, which is shorter than its diff:
```python
import functools
import math

import jax
import jax.numpy as jnp
import ml_dtypes
import numpy as np
from jax import lax
from jax.experimental import pallas as pl
from jax.experimental.pallas import tpu as pltpu
from jax.sharding import PartitionSpec as P

INPUTS = 1024
FRAME = 1536
TAPS = 4
BLOCK = 128
VMEM_LIMIT = 56 * 1024 * 1024


def pfb_window(frame_len, taps):
    total = taps * frame_len
    position = np.arange(total, dtype=np.float64)
    centred = (position - total / 2 + 0.5) / frame_len
    taper = 0.54 - 0.46 * np.cos(2.0 * math.pi * position / (total - 1))
    return (np.sinc(centred) * taper).reshape(taps, frame_len).astype(np.float32)


def dft_table(frame_len):
    channels = frame_len // 2
    phase = np.arange(channels)[:, None] * np.arange(frame_len)[None, :] % frame_len
    angle = 2.0 * math.pi / frame_len * phase
    table = np.stack([np.cos(angle), -np.sin(angle)]) / math.sqrt(frame_len)
    return table.astype(np.float32)


def chunk_sizes(count):
    if count % 6 == 0 and count >= 12:
        unit = count // 6
        return [unit, 2 * unit, 2 * unit, unit]
    return [1] * count if count <= 3 else [count // 2, count - count // 2]


def dft_kernel(group, spectra, gain_ref, table_ref, filt_ref, *refs):
    out_ref, turn_ref = refs[-2:]
    half = table_ref.shape[0] // 2
    first = pl.program_id(0) * group
    for pair in range(group // 2):
        rows = filt_ref[pl.ds(pair * 2 * spectra, 2 * spectra), :]
        spectrum = lax.dot_general(
            table_ref[...],
            rows,
            (((1,), (1,)), ((), ())),
            preferred_element_type=jnp.float32,
        )
        for sub in range(2):
            idx = pair * 2 + sub
            gain = gain_ref[first + idx]
            for part in range(2):
                piece = spectrum[
                    part * half : (part + 1) * half, sub * spectra : (sub + 1) * spectra
                ]
                turn_ref[part, pl.ds(idx, half, stride=group), :] = piece * gain
    for part in range(2):
        out_ref[:, :, part * spectra : (part + 1) * spectra] = (
            turn_ref[part].reshape(half, group, spectra).astype(out_ref.dtype)
        )


def dft(filtered, table, gain, local_inputs, spectra, earlier):
    rows, frame_len = table.shape
    half = rows // 2
    group = min(16, local_inputs)
    return pl.pallas_call(
        functools.partial(dft_kernel, group, spectra),
        grid=(local_inputs // group,),
        out_shape=jax.ShapeDtypeStruct((half, local_inputs, 2 * spectra), jnp.bfloat16),
        in_specs=[
            pl.BlockSpec(memory_space=pltpu.SMEM),
            pl.BlockSpec((rows, frame_len), lambda g: (0, 0)),
            pl.BlockSpec((group * spectra, frame_len), lambda g: (g, 0)),
        ]
        + [pl.BlockSpec(memory_space=pl.ANY)] * len(earlier),
        out_specs=pl.BlockSpec((half, group, 2 * spectra), lambda g: (0, g, 0)),
        scratch_shapes=[pltpu.VMEM((2, half * group, spectra), jnp.float32)],
        compiler_params=pltpu.CompilerParams(vmem_limit_bytes=VMEM_LIMIT),
        cost_estimate=pl.CostEstimate(
            flops=2 * rows * frame_len * local_inputs * spectra,
            bytes_accessed=2 * (rows * frame_len + local_inputs * spectra * (frame_len + rows)),
            transcendentals=0,
        ),
        name="dft",
    )(gain, table, filtered, *earlier)


def gram_kernel(samples_per_chan, spectra, *refs):
    recv_ref, out_ref = refs[0], refs[-1]
    num_dev, _, local_inputs, width = recv_ref.shape
    inputs = num_dev * local_inputs
    nblk = inputs // BLOCK
    chan = recv_ref[...].reshape(inputs, width)
    wide = chan.astype(jnp.float32)
    power = jnp.sum(wide * wide)
    scale = 1.0 / (power / samples_per_chan + 1e-06) / spectra
    turned = jnp.concatenate([-chan[:, spectra:], chan[:, :spectra]], axis=1)
    pair_of = {}
    for row in range(nblk):
        for col in range(row, nblk):
            pair_of[row, col] = len(pair_of)
    span = 2 if nblk % 2 == 0 else 1
    for col in range(0, nblk, span):
        left = chan[: (col + span) * BLOCK]
        for part, source in enumerate((chan, turned)):
            right = source[col * BLOCK : (col + span) * BLOCK]
            product = lax.dot_general(
                left, right, (((1,), (1,)), ((), ())), preferred_element_type=jnp.float32
            )
            product = (product * scale).astype(out_ref.dtype)
            for sub in range(span):
                for row in range(col + sub + 1):
                    out_ref[0, pair_of[row, col + sub], part] = product[
                        row * BLOCK : (row + 1) * BLOCK, sub * BLOCK : (sub + 1) * BLOCK
                    ]


def gram(received, earlier, start, total, spectra):
    num_dev, count, local_inputs, width = received.shape
    nblk = num_dev * local_inputs // BLOCK
    pairs = nblk * (nblk + 1) // 2
    out_shape = jax.ShapeDtypeStruct((total, pairs, 2, BLOCK, BLOCK), jnp.bfloat16)
    in_specs = [pl.BlockSpec((num_dev, 1, local_inputs, width), lambda k: (0, k, 0, 0))]
    args = [received]
    aliases = {}
    if earlier is not None:
        in_specs.append(pl.BlockSpec(memory_space=pl.ANY))
        args.append(earlier)
        aliases = {1: 0}
    return pl.pallas_call(
        functools.partial(gram_kernel, INPUTS * spectra, spectra),
        grid=(count,),
        out_shape=out_shape,
        in_specs=in_specs,
        out_specs=pl.BlockSpec((1, pairs, 2, BLOCK, BLOCK), lambda k: (start + k, 0, 0, 0, 0)),
        input_output_aliases=aliases,
        compiler_params=pltpu.CompilerParams(vmem_limit_bytes=VMEM_LIMIT),
        cost_estimate=pl.CostEstimate(
            flops=count * pairs * 4 * BLOCK * BLOCK * width,
            bytes_accessed=count * (pairs * 4 * BLOCK * BLOCK + 2 * width * num_dev * local_inputs),
            transcendentals=0,
        ),
        name="gram",
    )(*args)


def local(samples, input_gain):
    num_dev = lax.axis_size("dev")
    local_inputs = samples.shape[0]
    channels = FRAME // 2
    spectra = samples.shape[1] // FRAME - TAPS + 1
    local_chans = channels // num_dev
    window = jnp.asarray(pfb_window(FRAME, TAPS))
    table = dft_table(FRAME).reshape(2, num_dev, local_chans, FRAME)
    frames = samples.reshape(local_inputs, spectra + TAPS - 1, FRAME)
    acc = jnp.zeros((local_inputs, spectra, FRAME), jnp.float32)
    for tap in range(TAPS):
        acc = acc + window[tap][None, None, :] * frames[:, tap : tap + spectra, :].astype(
            jnp.float32
        )
    filtered = acc.astype(jnp.bfloat16).reshape(local_inputs * spectra, FRAME)
    visibility = None
    start = 0
    arrived = []
    before = []
    for count in chunk_sizes(local_chans):
        part = table[:, :, start : start + count].reshape(2 * num_dev * count, FRAME)
        part = jnp.asarray(part.astype(ml_dtypes.bfloat16))
        before = dft(filtered, part, input_gain, local_inputs, spectra, before)
        outgoing = before.reshape(num_dev, count, local_inputs, 2 * spectra)
        before = [before]
        received = lax.all_to_all(outgoing, "dev", split_axis=0, concat_axis=0, tiled=True)
        arrived.append((start, received))
        start += count
    for start, received in arrived:
        visibility = gram(received, visibility, start, local_chans, spectra)
    return visibility


def solution(mesh):
    in_specs = (P("dev", None), P("dev"))
    out_specs = P("dev", None, None, None, None)
    return jax.shard_map(local, mesh=mesh, in_specs=in_specs, out_specs=out_specs, check_vma=False)
```

time: 816 us -> 366 us (0.45)
  local copies, waits for them, and re-layouts: 203 us -> 13.9 us
  matrix products: 153 us -> 0 us
  other arithmetic: 134 us -> 29.2 us
  Pallas kernels: 0 us -> 85.7 us
  waiting for transfers between devices: 279 us -> 216 us
  blocking collectives: 42.2 us -> 0 us
  starting transfers between devices: 4.51 us -> 19.6 us
    dot_general x3 -> x0, matrix products: 153 us -> none  [the longest x1 56.1 us: correlate(): jnp.einsum('kpis,kpjs->kpij', left, turned, preferred_element_type=jnp.fl...]
    pallas_call x0 -> x8, Pallas kernels: none -> 85.7 us  [the longest x4 44.6 us: dft(): pl.pallas_call(functools.partial(dft_kernel, group, spectra), grid=(local...]
    gather x3 -> x0, local copies, waits for them, and re-layouts: 85.6 us -> none  [the longest x2 62 us: correlate(): right = jnp.take(tiles, cols_idx, axis=1)]
    all_to_all x1 -> x4, waiting for transfers between devices: 279 us -> 216 us  [local(): lax.all_to_all(outgoing, 'dev', split_axis=0, concat_axis=0, tiled=True)]
    neg x2 -> x0, other arithmetic: 57.4 us -> none  [the longest x1 37 us: correlate(): -right[..., spectra:]]
    convert_element_type x2 -> x0, local copies, waits for them, and re-layouts: 54.4 us -> none  [the longest x1 37.9 us: correlate(): return stacked.astype(jnp.bfloat16)]
    convert_element_type x3 -> x1, other arithmetic: 76.5 us -> 29.2 us  [local(): filtered = acc.astype(jnp.bfloat16).reshape(local_inputs * spectra, FRAME)]
    psum x1 -> x0, blocking collectives: 42.2 us -> none  [local(): power = lax.psum(partial_power, 'dev')]
  transfers between devices with their start and end apart: 1 -> 4, of which waited for: 1 -> 4; matrix products, arithmetic and copies ran while one was open for 0% -> 0% of each run, Pallas kernels for 0% -> 19%
where the time goes in v1:
time: 366 us; the launch traced here: 365 us
  waiting for transfers between devices  216 us (59%)
  Pallas kernels  85.7 us (23%)
  other arithmetic  29.2 us (8%)
  starting transfers between devices  19.6 us (5%)
  local copies, waits for them, and re-layouts  13.9 us (4%)
    all_to_all x4, waiting for transfers between devices, local(): lax.all_to_all(outgoing, 'dev', split_axis=0, concat_axis=0, tiled=True)  216 us
    pallas_call x4, Pallas kernels, dft(): pl.pallas_call(functools.partial(dft_kernel, group, spectra), grid=(local...  44.6 us
    pallas_call x4, Pallas kernels, gram(): pl.pallas_call(functools.partial(gram_kernel, INPUTS * spectra, spectra),...  41.1 us
    convert_element_type x1, other arithmetic, local(): filtered = acc.astype(jnp.bfloat16).reshape(local_inputs * spectra, FRAME)  29.2 us
    all_to_all x4, starting transfers between devices, local(): lax.all_to_all(outgoing, 'dev', split_axis=0, concat_axis=0, tiled=True)  19.6 us
    reshape x1, local copies, waits for them, and re-layouts, local(): frames = samples.reshape(local_inputs, spectra + TAPS - 1, FRAME)  12.5 us
  transfers between devices with their start and end apart: 4, of which 4 were waited for; matrix products, arithmetic and copies ran while one was open for 0% of the time, Pallas kernels for 19%

profile of v1, /device:TPU:0, one launch (start us, length us, event | category | flops | bytes accessed | tf_op | source)
XLA Modules:
  0.0 364.5 jit_solution(4669275834073647801)
XLA Ops:
  0.0 0.0 copy-start.2
  0.0 0.0 copy-start.3
  0.0 0.0 copy-start.4
  0.0 0.0 copy-start.5
  0.0 12.5 %reshape.22 = bf16[32,131,1536]{2,1,0:T(8,128)(2,1)} reshape(bf16[32,201216]{1,0:T(8,128)(2,1)} %param.7) | data formatting | bytes 25755648 | tf_op jit(solution)/shard_map/reshape | solution.py:162
  12.6 0.0 copy-done.2
  12.6 0.0 copy-done.3
  12.6 0.0 copy-done.4
  12.6 0.0 copy-done.5
  12.6 29.2 %add_convert_fusion = bf16[32,128,1536]{2,1,0:T(8,128)(2,1)} fusion(bf16[32,131,1536]{2,1,0:T(8,128)(2,1)} %reshape.22, f32[1536]{0:T(1024)S(1)} %copy-done.2, f32[1536]{0:T(1024)S(1)} %copy-done.3, f32[1536]{0:T(1024)S(1)} %copy-done.4, f32[1536]{0:T(1024)S(1)} %copy-done.5), kind=kLoop, calls=%fused_computation | loop fusion | flops 75497472 | bytes 62939136 | tf_op jit(solution)/shard_map/convert_element_type | solution.py:168
  41.8 8.7 %dft.4.refs_0_ = bf16[128,32,256]{2,1,0:T(8,128)(2,1)} custom-call(f32[32]{0:T(128)} %gain_ref.7, bf16[256,1536]{1,0:T(8,128)(2,1)} %constant.11.clone.table_ref, bf16[4096,1536]{1,0:T(8,128)(2,1)} %bitcast.5), custom_call_target="tpu_custom_call" | custom-call | flops 3221225472 | bytes 15466496 | tf_op jit(solution)/shard_map/dft/pallas_call | solution.py:73
  50.5 7.3 %all-to-all-start.3 = ((bf16[32,4,32,256]{3,2,1,0:T(8,128)(2,1)}), bf16[32,4,32,256]{3,2,1,0:T(8,128)(2,1)S(1)}, u32[]{:S(2)}, u32[]{:S(2)}) async-start(bf16[32,4,32,256]{3,2,1,0:T(8,128)(2,1)} %bitcast.10), calls=%async_computation.3 | async-start | bytes 4194304 | tf_op jit(solution)/shard_map/all_to_all | solution.py:179
  57.8 13.6 %dft.5.refs_0_ = bf16[256,32,256]{2,1,0:T(8,128)(2,1)} custom-call(f32[32]{0:T(128)} %gain_ref.7, bf16[512,1536]{1,0:T(8,128)(2,1)} %constant.12.clone.table_ref, bf16[4096,1536]{1,0:T(8,128)(2,1)} %bitcast.6, bf16[128,32,256]{2,1,0:T(8,128)(2,1)} %dft.4.refs_0_), custom_call_target="tpu_custom_call" | custom-call | flops 6442450944 | bytes 18350080 | tf_op jit(solution)/shard_map/dft/pallas_call | solution.py:73
  71.4 35.3 %all-to-all-done.3.refs_0_ = bf16[32,4,32,256]{3,2,1,0:T(8,128)(2,1)S(1)} async-done(((bf16[32,4,32,256]{3,2,1,0:T(8,128)(2,1)}), bf16[32,4,32,256]{3,2,1,0:T(8,128)(2,1)S(1)}, u32[]{:S(2)}, u32[]{:S(2)}) %all-to-all-start.3) | async-done | bytes 2097184 | tf_op jit(solution)/shard_map/all_to_all | solution.py:179
  106.7 0.0 copy-start.1
  106.7 4.3 %all-to-all-start.2 = ((bf16[32,8,32,256]{3,2,1,0:T(8,128)(2,1)}), bf16[32,8,32,256]{3,2,1,0:T(8,128)(2,1)}, u32[]{:S(2)}, u32[]{:S(2)}) async-start(bf16[32,8,32,256]{3,2,1,0:T(8,128)(2,1)} %bitcast.12), calls=%async_computation.2 | async-start | bytes 8388608 | tf_op jit(solution)/shard_map/all_to_all | solution.py:179
  111.0 13.6 %dft.6.refs_0_ = bf16[256,32,256]{2,1,0:T(8,128)(2,1)} custom-call(f32[32]{0:T(128)} %gain_ref.7, bf16[512,1536]{1,0:T(8,128)(2,1)} %constant.13.clone.table_ref, bf16[4096,1536]{1,0:T(8,128)(2,1)} %bitcast.7, bf16[256,32,256]{2,1,0:T(8,128)(2,1)} %dft.5.refs_0_), custom_call_target="tpu_custom_call" | custom-call | flops 6442450944 | bytes 18350080 | tf_op jit(solution)/shard_map/dft/pallas_call | solution.py:73
  124.6 80.2 %all-to-all-done.2.refs_0_ = bf16[32,8,32,256]{3,2,1,0:T(8,128)(2,1)} async-done(((bf16[32,8,32,256]{3,2,1,0:T(8,128)(2,1)}), bf16[32,8,32,256]{3,2,1,0:T(8,128)(2,1)}, u32[]{:S(2)}, u32[]{:S(2)}) %all-to-all-start.2) | async-done | bytes 4194336 | tf_op jit(solution)/shard_map/all_to_all | solution.py:179
  204.8 4.0 %all-to-all-start.1 = ((bf16[32,8,32,256]{3,2,1,0:T(8,128)(2,1)}), bf16[32,8,32,256]{3,2,1,0:T(8,128)(2,1)}, u32[]{:S(2)}, u32[]{:S(2)}) async-start(bf16[32,8,32,256]{3,2,1,0:T(8,128)(2,1)} %bitcast.9), calls=%async_computation.1 | async-start | bytes 8388608 | tf_op jit(solution)/shard_map/all_to_all | solution.py:179
  208.8 8.7 %dft.7 = bf16[128,32,256]{2,1,0:T(8,128)(2,1)} custom-call(f32[32]{0:T(128)} %gain_ref.7, bf16[256,1536]{1,0:T(8,128)(2,1)} %constant.14.clone.table_ref, bf16[4096,1536]{1,0:T(8,128)(2,1)} %bitcast.8, bf16[256,32,256]{2,1,0:T(8,128)(2,1)} %dft.6.refs_0_), custom_call_target="tpu_custom_call" | custom-call | flops 3221225472 | bytes 15466496 | tf_op jit(solution)/shard_map/dft/pallas_call | solution.py:73
  217.6 0.0 copy-done.1
  217.6 85.1 %all-to-all-done.1.refs_0_ = bf16[32,8,32,256]{3,2,1,0:T(8,128)(2,1)} async-done(((bf16[32,8,32,256]{3,2,1,0:T(8,128)(2,1)}), bf16[32,8,32,256]{3,2,1,0:T(8,128)(2,1)}, u32[]{:S(2)}, u32[]{:S(2)}) %all-to-all-start.1) | async-done | bytes 4194336 | tf_op jit(solution)/shard_map/all_to_all | solution.py:179
  302.7 4.0 %all-to-all-start = ((bf16[32,4,32,256]{3,2,1,0:T(8,128)(2,1)}), bf16[32,4,32,256]{3,2,1,0:T(8,128)(2,1)S(1)}, u32[]{:S(2)}, u32[]{:S(2)}) async-start(bf16[32,4,32,256]{3,2,1,0:T(8,128)(2,1)} %bitcast.11), calls=%async_computation | async-start | bytes 4194304 | tf_op jit(solution)/shard_map/all_to_all | solution.py:179
  306.7 7.6 %gram.4.refs_1_ = bf16[24,36,2,128,128]{4,3,2,1,0:T(8,128)(2,1)} custom-call(bf16[32,4,32,256]{3,2,1,0:T(8,128)(2,1)} %copy-done.1), custom_call_target="tpu_custom_call" | custom-call | flops 2415919104 | bytes 11534336 | tf_op jit(solution)/shard_map/gram/pallas_call | solution.py:137
  314.3 12.9 %gram.5.refs_1_ = bf16[24,36,2,128,128]{4,3,2,1,0:T(8,128)(2,1)} custom-call(bf16[32,8,32,256]{3,2,1,0:T(8,128)(2,1)} %all-to-all-done.2.refs_0_, bf16[24,36,2,128,128]{4,3,2,1,0:T(8,128)(2,1)} %gram.4.refs_1_), custom_call_target="tpu_custom_call", output_to_operand_aliasing={{}: (1, {})} | custom-call | flops 4831838208 | bytes 23068672 | tf_op jit(solution)/shard_map/gram/pallas_call | solution.py:137
  327.2 12.9 %gram.6.refs_1_ = bf16[24,36,2,128,128]{4,3,2,1,0:T(8,128)(2,1)} custom-call(bf16[32,8,32,256]{3,2,1,0:T(8,128)(2,1)} %all-to-all-done.1.refs_0_, bf16[24,36,2,128,128]{4,3,2,1,0:T(8,128)(2,1)} %gram.5.refs_1_), custom_call_target="tpu_custom_call", output_to_operand_aliasing={{}: (1, {})} | custom-call | flops 4831838208 | bytes 23068672 | tf_op jit(solution)/shard_map/gram/pallas_call | solution.py:137
  340.1 15.4 %all-to-all-done.refs_0_ = bf16[32,4,32,256]{3,2,1,0:T(8,128)(2,1)S(1)} async-done(((bf16[32,4,32,256]{3,2,1,0:T(8,128)(2,1)}), bf16[32,4,32,256]{3,2,1,0:T(8,128)(2,1)S(1)}, u32[]{:S(2)}, u32[]{:S(2)}) %all-to-all-start) | async-done | bytes 2097184 | tf_op jit(solution)/shard_map/all_to_all | solution.py:179
  355.6 0.0 copy-start
  355.6 1.3 copy-done
  356.9 7.6 %gram.7 = bf16[24,36,2,128,128]{4,3,2,1,0:T(8,128)(2,1)} custom-call(bf16[32,4,32,256]{3,2,1,0:T(8,128)(2,1)} %copy-done, bf16[24,36,2,128,128]{4,3,2,1,0:T(8,128)(2,1)} %gram.6.refs_1_), custom_call_target="tpu_custom_call", output_to_operand_aliasing={{}: (1, {})} | custom-call | flops 2415919104 | bytes 11534336 | tf_op jit(solution)/shard_map/gram/pallas_call | solution.py:137
Async XLA Ops:
  0.0 12.6 %copy-start.2 = (f32[1536]{0:T(1024)S(1)}, f32[1536]{0:T(1024)}, u32[]{:S(2)}) copy-start(f32[1536]{0:T(1024)} %constant.22) | copy-start | bytes 18436
  0.0 12.6 %copy-start.3 = (f32[1536]{0:T(1024)S(1)}, f32[1536]{0:T(1024)}, u32[]{:S(2)}) copy-start(f32[1536]{0:T(1024)} %constant.20) | copy-start | bytes 18436
  0.0 12.6 %copy-start.4 = (f32[1536]{0:T(1024)S(1)}, f32[1536]{0:T(1024)}, u32[]{:S(2)}) copy-start(f32[1536]{0:T(1024)} %constant.18) | copy-start | bytes 18436
  0.0 12.6 %copy-start.5 = (f32[1536]{0:T(1024)S(1)}, f32[1536]{0:T(1024)}, u32[]{:S(2)}) copy-start(f32[1536]{0:T(1024)} %constant.16) | copy-start | bytes 18436
  50.5 56.2 %all-to-all-start.3 = ((bf16[32,4,32,256]{3,2,1,0:T(8,128)(2,1)}), bf16[32,4,32,256]{3,2,1,0:T(8,128)(2,1)S(1)}, u32[]{:S(2)}, u32[]{:S(2)}) async-start(bf16[32,4,32,256]{3,2,1,0:T(8,128)(2,1)} %bitcast.10), calls=%async_computation.3 | async-start | bytes 4194304 | tf_op jit(solution)/shard_map/all_to_all | solution.py:179
  106.7 110.9 %copy-start.1 = (bf16[32,4,32,256]{3,2,1,0:T(8,128)(2,1)}, bf16[32,4,32,256]{3,2,1,0:T(8,128)(2,1)S(1)}, u32[]{:S(2)}) copy-start(bf16[32,4,32,256]{3,2,1,0:T(8,128)(2,1)S(1)} %all-to-all-done.3.refs_0_) | copy-start | bytes 6291460
  106.7 98.1 %all-to-all-start.2 = ((bf16[32,8,32,256]{3,2,1,0:T(8,128)(2,1)}), bf16[32,8,32,256]{3,2,1,0:T(8,128)(2,1)}, u32[]{:S(2)}, u32[]{:S(2)}) async-start(bf16[32,8,32,256]{3,2,1,0:T(8,128)(2,1)} %bitcast.12), calls=%async_computation.2 | async-start | bytes 8388608 | tf_op jit(solution)/shard_map/all_to_all | solution.py:179
  204.8 97.9 %all-to-all-start.1 = ((bf16[32,8,32,256]{3,2,1,0:T(8,128)(2,1)}), bf16[32,8,32,256]{3,2,1,0:T(8,128)(2,1)}, u32[]{:S(2)}, u32[]{:S(2)}) async-start(bf16[32,8,32,256]{3,2,1,0:T(8,128)(2,1)} %bitcast.9), calls=%async_computation.1 | async-start | bytes 8388608 | tf_op jit(solution)/shard_map/all_to_all | solution.py:179
  302.7 52.9 %all-to-all-start = ((bf16[32,4,32,256]{3,2,1,0:T(8,128)(2,1)}), bf16[32,4,32,256]{3,2,1,0:T(8,128)(2,1)S(1)}, u32[]{:S(2)}, u32[]{:S(2)}) async-start(bf16[32,4,32,256]{3,2,1,0:T(8,128)(2,1)} %bitcast.11), calls=%async_computation | async-start | bytes 4194304 | tf_op jit(solution)/shard_map/all_to_all | solution.py:179
  355.6 1.3 copy-start

commit v2 on v1

--- a/solution.py
+++ b/solution.py
@@ -14,6 +14,7 @@
 FRAME = 1536
 TAPS = 4
 BLOCK = 128
+LANES = 128
 VMEM_LIMIT = 56 * 1024 * 1024
 
 
@@ -34,10 +35,64 @@
 
 
 def chunk_sizes(count):
-    if count % 6 == 0 and count >= 12:
-        unit = count // 6
-        return [unit, 2 * unit, 2 * unit, unit]
+    if count % 8 == 0:
+        unit = count // 8
+        return [unit, 6 * unit, unit]
     return [1] * count if count <= 3 else [count // 2, count - count // 2]
+
+
+def filter_kernel(spectra, frame_len, samples_ref, window_ref, out_ref, turn_ref):
+    group = samples_ref.shape[0]
+    base = pl.program_id(1) * out_ref.shape[1]
+
+    def columns(step, _):
+        inside = pl.multiple_of(step * LANES, LANES)
+        weights = [window_ref[tap : tap + 1, pl.ds(inside, LANES)] for tap in range(TAPS)]
+
+        def frame(idx):
+            at = pl.multiple_of(base + inside + idx * frame_len, LANES)
+            return samples_ref[:, pl.ds(at, LANES)].astype(jnp.float32)
+
+        held = [frame(idx) for idx in range(TAPS - 1)]
+        for spectrum in range(spectra):
+            held.append(frame(spectrum + TAPS - 1))
+            acc = held[0] * weights[0]
+            for tap in range(1, TAPS):
+                acc = acc + held[tap] * weights[tap]
+            turn_ref[step, pl.ds(spectrum, group, stride=spectra), :] = acc
+            held.pop(0)
+        return 0
+
+    lax.fori_loop(0, turn_ref.shape[0], columns, 0)
+    for step in range(turn_ref.shape[0]):
+        out_ref[:, step * LANES : (step + 1) * LANES] = turn_ref[
+            step, : group * spectra
+        ].astype(out_ref.dtype)
+
+
+def filterbank(samples, window, spectra):
+    local_inputs, length = samples.shape
+    frame_len = window.shape[1]
+    group = min(16, local_inputs)
+    width = frame_len // 3
+    return pl.pallas_call(
+        functools.partial(filter_kernel, spectra, frame_len),
+        grid=(local_inputs // group, frame_len // width),
+        out_shape=jax.ShapeDtypeStruct((local_inputs * spectra, frame_len), jnp.bfloat16),
+        in_specs=[
+            pl.BlockSpec((group, length), lambda g, j: (g, 0)),
+            pl.BlockSpec((TAPS, width), lambda g, j: (0, j)),
+        ],
+        out_specs=pl.BlockSpec((group * spectra, width), lambda g, j: (g, j)),
+        scratch_shapes=[pltpu.VMEM((width // LANES, (group + 1) * spectra, LANES), jnp.float32)],
+        compiler_params=pltpu.CompilerParams(vmem_limit_bytes=VMEM_LIMIT),
+        cost_estimate=pl.CostEstimate(
+            flops=2 * TAPS * local_inputs * spectra * frame_len,
+            bytes_accessed=2 * local_inputs * (length + spectra * frame_len),
+            transcendentals=0,
+        ),
+        name="filterbank",
+    )(samples, window)
 
 
 def dft_kernel(group, spectra, gain_ref, table_ref, filt_ref, *refs):
@@ -62,7 +117,7 @@
                 turn_ref[part, pl.ds(idx, half, stride=group), :] = piece * gain
     for part in range(2):
         out_ref[:, :, part * spectra : (part + 1) * spectra] = (
-            turn_ref[part].reshape(half, group, spectra).astype(out_ref.dtype)
+            turn_ref[part, : half * group].reshape(half, group, spectra).astype(out_ref.dtype)
         )
 
 
@@ -81,7 +136,7 @@
         ]
         + [pl.BlockSpec(memory_space=pl.ANY)] * len(earlier),
         out_specs=pl.BlockSpec((half, group, 2 * spectra), lambda g: (0, g, 0)),
-        scratch_shapes=[pltpu.VMEM((2, half * group, spectra), jnp.float32)],
+        scratch_shapes=[pltpu.VMEM((2, (half + 1) * group, spectra), jnp.float32)],
         compiler_params=pltpu.CompilerParams(vmem_limit_bytes=VMEM_LIMIT),
         cost_estimate=pl.CostEstimate(
             flops=2 * rows * frame_len * local_inputs * spectra,
@@ -159,13 +214,7 @@
     local_chans = channels // num_dev
     window = jnp.asarray(pfb_window(FRAME, TAPS))
     table = dft_table(FRAME).reshape(2, num_dev, local_chans, FRAME)
-    frames = samples.reshape(local_inputs, spectra + TAPS - 1, FRAME)
-    acc = jnp.zeros((local_inputs, spectra, FRAME), jnp.float32)
-    for tap in range(TAPS):
-        acc = acc + window[tap][None, None, :] * frames[:, tap : tap + spectra, :].astype(
-            jnp.float32
-        )
-    filtered = acc.astype(jnp.bfloat16).reshape(local_inputs * spectra, FRAME)
+    filtered = filterbank(samples, window, spectra)
     visibility = None
     start = 0
     arrived = []

time: 366 us -> 346 us (0.945)
  other arithmetic: 29.2 us -> 0 us
  Pallas kernels: 85.7 us -> 111 us
  local copies, waits for them, and re-layouts: 13.9 us -> 2.29 us
  starting transfers between devices: 19.6 us -> 14.1 us
    convert_element_type x1 -> x0, other arithmetic: 29.2 us -> none  [local(): filtered = acc.astype(jnp.bfloat16).reshape(local_inputs * spectra, FRAME)]
    pallas_call x0 -> x1, Pallas kernels: none -> 29 us  [filterbank(): pl.pallas_call(functools.partial(filter_kernel, spectra, frame_len), grid...]
    reshape x1 -> x0, local copies, waits for them, and re-layouts: 12.5 us -> none  [local(): frames = samples.reshape(local_inputs, spectra + TAPS - 1, FRAME)]
    all_to_all x4 -> x3, starting transfers between devices: 19.6 us -> 14.1 us  [local(): lax.all_to_all(outgoing, 'dev', split_axis=0, concat_axis=0, tiled=True)]
    pallas_call x4 -> x3, Pallas kernels: 41.1 us -> 38.7 us  [gram(): pl.pallas_call(functools.partial(gram_kernel, INPUTS * spectra, spectra),...]
    all_to_all x4 -> x3, waiting for transfers between devices: 216 us -> 217 us  [local(): lax.all_to_all(outgoing, 'dev', split_axis=0, concat_axis=0, tiled=True)]
    pallas_call x4 -> x3, Pallas kernels: 44.6 us -> 43.8 us  [dft(): pl.pallas_call(functools.partial(dft_kernel, group, spectra), grid=(local...]
  transfers between devices with their start and end apart: 4 -> 3, of which waited for: 4 -> 3; matrix products, arithmetic and copies ran while one was open for 0% -> 0% of each run, Pallas kernels for 19% -> 20%
where the time goes in v2:
time: 346 us; the launch traced here: 345 us
  waiting for transfers between devices  217 us (63%)
  Pallas kernels  111 us (32%)
  starting transfers between devices  14.1 us (4%)
    all_to_all x3, waiting for transfers between devices, local(): lax.all_to_all(outgoing, 'dev', split_axis=0, concat_axis=0, tiled=True)  217 us
    pallas_call x3, Pallas kernels, dft(): pl.pallas_call(functools.partial(dft_kernel, group, spectra), grid=(local...  43.8 us
    pallas_call x3, Pallas kernels, gram(): pl.pallas_call(functools.partial(gram_kernel, INPUTS * spectra, spectra),...  38.7 us
    pallas_call x1, Pallas kernels, filterbank(): pl.pallas_call(functools.partial(filter_kernel, spectra, frame_len), grid...  29 us
    all_to_all x3, starting transfers between devices, local(): lax.all_to_all(outgoing, 'dev', split_axis=0, concat_axis=0, tiled=True)  14.1 us
  transfers between devices with their start and end apart: 3, of which 3 were waited for; matrix products, arithmetic and copies ran while one was open for 0% of the time, Pallas kernels for 20%

profile of v2, /device:TPU:0, one launch (start us, length us, event | category | flops | bytes accessed | tf_op | source)
XLA Modules:
  0.0 345.1 jit_solution(3849813642574989429)
XLA Ops:
  0.0 29.0 %filterbank.1.filt_ref = bf16[4096,1536]{1,0:T(8,128)(2,1)} custom-call(bf16[32,201216]{1,0:T(8,128)(2,1)} %samples_ref.1, f32[4,1536]{1,0:T(4,128)} %constant.8.clone.window_ref), custom_call_target="tpu_custom_call" | custom-call | flops 50331648 | bytes 25460736 | tf_op jit(solution)/shard_map/filterbank/pallas_call | solution.py:78
  29.0 8.8 %dft.3.refs_0_ = bf16[96,32,256]{2,1,0:T(8,128)(2,1)} custom-call(f32[32]{0:T(128)} %gain_ref.5, bf16[192,1536]{1,0:T(8,128)(2,1)} %constant.9.clone.table_ref, bf16[4096,1536]{1,0:T(8,128)(2,1)} %filterbank.1.filt_ref), custom_call_target="tpu_custom_call" | custom-call | flops 2415919104 | bytes 14745600 | tf_op jit(solution)/shard_map/dft/pallas_call | solution.py:128
  37.9 7.3 %all-to-all-start.2 = ((bf16[32,3,32,256]{3,2,1,0:T(8,128)(2,1)}), bf16[32,3,32,256]{3,2,1,0:T(8,128)(2,1)S(1)}, u32[]{:S(2)}, u32[]{:S(2)}) async-start(bf16[32,3,32,256]{3,2,1,0:T(8,128)(2,1)} %bitcast.4), calls=%async_computation.2 | async-start | bytes 3145728 | tf_op jit(solution)/shard_map/all_to_all | solution.py:228
  45.2 26.1 %dft.4.refs_0_ = bf16[576,32,256]{2,1,0:T(8,128)(2,1)} custom-call(f32[32]{0:T(128)} %gain_ref.5, bf16[1152,1536]{1,0:T(8,128)(2,1)} %constant.10.clone.table_ref, bf16[4096,1536]{1,0:T(8,128)(2,1)} %filterbank.1.filt_ref, bf16[96,32,256]{2,1,0:T(8,128)(2,1)} %dft.3.refs_0_), custom_call_target="tpu_custom_call" | custom-call | flops 14495514624 | bytes 25559040 | tf_op jit(solution)/shard_map/dft/pallas_call | solution.py:128
  71.3 11.7 %all-to-all-done.2.refs_0_ = bf16[32,3,32,256]{3,2,1,0:T(8,128)(2,1)S(1)} async-done(((bf16[32,3,32,256]{3,2,1,0:T(8,128)(2,1)}), bf16[32,3,32,256]{3,2,1,0:T(8,128)(2,1)S(1)}, u32[]{:S(2)}, u32[]{:S(2)}) %all-to-all-start.2) | async-done | bytes 1572896 | tf_op jit(solution)/shard_map/all_to_all | solution.py:228
  82.9 0.0 copy-start.1
  82.9 1.1 copy-done.1
  84.1 3.9 %all-to-all-start.1 = ((bf16[32,18,32,256]{3,2,1,0:T(8,128)(2,1)}), bf16[32,18,32,256]{3,2,1,0:T(8,128)(2,1)}, u32[]{:S(2)}, u32[]{:S(2)}) async-start(bf16[32,18,32,256]{3,2,1,0:T(8,128)(2,1)} %bitcast.3), calls=%async_computation.1 | async-start | bytes 18874368 | tf_op jit(solution)/shard_map/all_to_all | solution.py:228
  88.0 8.9 %dft.5 = bf16[96,32,256]{2,1,0:T(8,128)(2,1)} custom-call(f32[32]{0:T(128)} %gain_ref.5, bf16[192,1536]{1,0:T(8,128)(2,1)} %constant.11.clone.table_ref, bf16[4096,1536]{1,0:T(8,128)(2,1)} %filterbank.1.filt_ref, bf16[576,32,256]{2,1,0:T(8,128)(2,1)} %dft.4.refs_0_), custom_call_target="tpu_custom_call" | custom-call | flops 2415919104 | bytes 14745600 | tf_op jit(solution)/shard_map/dft/pallas_call | solution.py:128
  96.8 200.3 %all-to-all-done.1.refs_0_ = bf16[32,18,32,256]{3,2,1,0:T(8,128)(2,1)} async-done(((bf16[32,18,32,256]{3,2,1,0:T(8,128)(2,1)}), bf16[32,18,32,256]{3,2,1,0:T(8,128)(2,1)}, u32[]{:S(2)}, u32[]{:S(2)}) %all-to-all-start.1) | async-done | bytes 9437216 | tf_op jit(solution)/shard_map/all_to_all | solution.py:228
  297.1 2.9 all-to-all-start
  300.0 6.2 %gram.3.refs_1_ = bf16[24,36,2,128,128]{4,3,2,1,0:T(8,128)(2,1)} custom-call(bf16[32,3,32,256]{3,2,1,0:T(8,128)(2,1)} %copy-done.1), custom_call_target="tpu_custom_call" | custom-call | flops 1811939328 | bytes 8650752 | tf_op jit(solution)/shard_map/gram/pallas_call | solution.py:192
  306.2 26.2 %gram.4.refs_1_ = bf16[24,36,2,128,128]{4,3,2,1,0:T(8,128)(2,1)} custom-call(bf16[32,18,32,256]{3,2,1,0:T(8,128)(2,1)} %all-to-all-done.1.refs_0_, bf16[24,36,2,128,128]{4,3,2,1,0:T(8,128)(2,1)} %gram.3.refs_1_), custom_call_target="tpu_custom_call", output_to_operand_aliasing={{}: (1, {})} | custom-call | flops 10871635968 | bytes 51904512 | tf_op jit(solution)/shard_map/gram/pallas_call | solution.py:192
  332.5 5.3 %all-to-all-done.refs_0_ = bf16[32,3,32,256]{3,2,1,0:T(8,128)(2,1)S(1)} async-done(((bf16[32,3,32,256]{3,2,1,0:T(8,128)(2,1)}), bf16[32,3,32,256]{3,2,1,0:T(8,128)(2,1)S(1)}, u32[]{:S(2)}, u32[]{:S(2)}) %all-to-all-start) | async-done | bytes 1572896 | tf_op jit(solution)/shard_map/all_to_all | solution.py:228
  337.7 0.0 copy-start
  337.7 1.1 copy-done
  338.9 6.2 %gram.5 = bf16[24,36,2,128,128]{4,3,2,1,0:T(8,128)(2,1)} custom-call(bf16[32,3,32,256]{3,2,1,0:T(8,128)(2,1)} %copy-done, bf16[24,36,2,128,128]{4,3,2,1,0:T(8,128)(2,1)} %gram.4.refs_1_), custom_call_target="tpu_custom_call", output_to_operand_aliasing={{}: (1, {})} | custom-call | flops 1811939328 | bytes 8650752 | tf_op jit(solution)/shard_map/gram/pallas_call | solution.py:192
Async XLA Ops:
  37.9 45.0 %all-to-all-start.2 = ((bf16[32,3,32,256]{3,2,1,0:T(8,128)(2,1)}), bf16[32,3,32,256]{3,2,1,0:T(8,128)(2,1)S(1)}, u32[]{:S(2)}, u32[]{:S(2)}) async-start(bf16[32,3,32,256]{3,2,1,0:T(8,128)(2,1)} %bitcast.4), calls=%async_computation.2 | async-start | bytes 3145728 | tf_op jit(solution)/shard_map/all_to_all | solution.py:228
  82.9 1.1 copy-start.1
  84.1 213.1 %all-to-all-start.1 = ((bf16[32,18,32,256]{3,2,1,0:T(8,128)(2,1)}), bf16[32,18,32,256]{3,2,1,0:T(8,128)(2,1)}, u32[]{:S(2)}, u32[]{:S(2)}) async-start(bf16[32,18,32,256]{3,2,1,0:T(8,128)(2,1)} %bitcast.3), calls=%async_computation.1 | async-start | bytes 18874368 | tf_op jit(solution)/shard_map/all_to_all | solution.py:228
  297.1 40.6 %all-to-all-start = ((bf16[32,3,32,256]{3,2,1,0:T(8,128)(2,1)}), bf16[32,3,32,256]{3,2,1,0:T(8,128)(2,1)S(1)}, u32[]{:S(2)}, u32[]{:S(2)}) async-start(bf16[32,3,32,256]{3,2,1,0:T(8,128)(2,1)} %bitcast.5), calls=%async_computation | async-start | bytes 3145728 | tf_op jit(solution)/shard_map/all_to_all | solution.py:228
  337.7 1.1 copy-start
